TPU v7x, 256 devices: a whole 4x4x8 slice. The times are simulated.
256 devices in a mesh: dp: 4 (over x_lo, core), eig: 64 (over z, x_hi, y).
Axes of the slice: x: 4 (x_hi: 2, x_lo: 2; x = x_hi * 2 + x_lo), y: 4, z: 8, core: 2. Of those that a mesh axis runs over, the one named last changes fastest.
Arguments:
- activations: bfloat16 [8192, 5120], P(('dp', 'eig')), may hold values from -6 to 6
- out_grads: bfloat16 [13824, 8192], P('eig', 'dp'), may hold values from -6 to 6
- basis_in: bfloat16 [5120, 5120], P('eig'), may hold values from -0.078125 to 0.078125
- basis_out: bfloat16 [13824, 13824], P('eig'), may hold values from -0.0546875 to 0.0546875
- block_ids: int32 [8], replicated, may hold values from 0 to 107, as said below
- seq_lens: int32 [8], P('dp'), may hold values from 128 to 1024, as said below
- query_grads: bfloat16 [32, 5120, 1024], P('dp', 'eig'), may hold values from -7.6293945e-05 to 7.6293945e-05
Outputs:
- scores: float32 [8, 32], P(None, 'dp')
Inputs may be any that keep to these rules, and one draw needn't show every extreme that they name: `block_ids`: distinct block numbers; blocks of 128 columns of basis_out. `seq_lens`: slots of a sequence from its count on are padding.
All inputs are finite; a program needn't handle non-finite values.
Results may differ from a plain program's by a relative error of at most 0.0052.
Values may be sent and summed in bfloat16 or wider, within the bound.
No kernel may reach another device: no remote copies, remote signals or barrier semaphores. Data moves between devices by JAX's collectives and lax.ppermute only.
A program may use at most 128 MiB of HBM per device.

v0:
```python
import jax
import jax.numpy as jnp
from jax import lax
from jax.sharding import PartitionSpec as P

BLOCK = 128
NSEL = 8
LEN = 1024


def per_device(activations, out_grads, basis_in, basis_out, block_ids, seq_lens, query_grads):
    rotated_act = lax.dot_general(
        basis_in,
        lax.all_gather(activations, "eig", axis=0, tiled=True),
        (((1,), (1,)), ((), ())),
        preferred_element_type=jnp.float32,
    ).astype(jnp.bfloat16)
    chosen_basis = jnp.concatenate(
        [
            lax.dynamic_slice_in_dim(basis_out, block_ids[number] * BLOCK, BLOCK, 1)
            for number in range(NSEL)
        ],
        axis=1,
    )
    width = chosen_basis.shape[1]
    summed_grad = lax.psum(
        lax.dot_general(
            chosen_basis, out_grads, (((0,), (0,)), ((), ())), preferred_element_type=jnp.float32
        ),
        "eig",
    ).astype(jnp.bfloat16)
    seq_count = seq_lens.shape[0]
    live_slots = lax.broadcasted_iota(jnp.int32, (seq_count, LEN), 1) < seq_lens[:, None]
    rotated_grad = jnp.where(
        live_slots.reshape(1, seq_count * LEN), summed_grad, jnp.zeros((), jnp.bfloat16)
    )
    grad_blocks = rotated_grad.reshape(width, seq_count, LEN)
    act_blocks = rotated_act.reshape(rotated_act.shape[0], seq_count, LEN)
    seq_grads = jnp.einsum(
        "ksl,isl->sik", grad_blocks, act_blocks, preferred_element_type=jnp.float32
    ).astype(jnp.bfloat16)
    every_seq = lax.all_gather(seq_grads, "dp", axis=0, tiled=True)
    partial_scores = jnp.einsum(
        "sik,qik->sq", every_seq, query_grads, preferred_element_type=jnp.float32
    )
    return lax.psum(partial_scores, "eig")


def solution(mesh):
    in_specs = (
        P(("dp", "eig"), None),
        P("eig", "dp"),
        P("eig", None),
        P("eig", None),
        P(),
        P("dp"),
        P("dp", "eig", None),
    )
    out_specs = P(None, "dp")
    return jax.shard_map(
        per_device, mesh=mesh, in_specs=in_specs, out_specs=out_specs, check_vma=False
    )
```

profile of v0, /device:TPU:2, one launch (start us, length us, event | category | flops | bytes accessed | tf_op | source)
XLA Modules:
  0.0 722.4 jit_solution(18155666218534469740)
XLA Ops:
  6.5 0.0 copy-start
  6.5 0.0 all-gather.3.cloned.1.call-start
  6.5 0.7 all-gather.3.cloned.1.call-update
  7.3 0.0 all-gather.5.cloned.1.call-start
  7.3 1.6 fusion.10
  14.0 0.7 iota_compare_fusion
  14.7 0.8 dynamic-slice_dynamic-update-slice_fusion.7
  15.6 0.8 dynamic-slice_dynamic-update-slice_fusion.6
  16.4 0.8 dynamic-slice_dynamic-update-slice_fusion.5
  17.3 0.8 dynamic-slice_dynamic-update-slice_fusion.4
  18.1 0.8 dynamic-slice_dynamic-update-slice_fusion.3
  18.9 0.8 dynamic-slice_dynamic-update-slice_fusion.2
  19.8 0.8 dynamic-slice_dynamic-update-slice_fusion.1
  20.6 0.8 dynamic-slice_dynamic-update-slice_fusion
  21.5 5.8 fusion.11
  27.2 455.1 %all-reduce.1 = bf16[1024,2048]{1,0:T(8,128)(2,1)} all-reduce(f32[1024,2048]{1,0:T(8,128)} %fusion.11), channel_id=1, replica_groups=mesh['dp'=4,'eig'=64] {'eig'}, use_global_device_ids=true, to_apply=%region_0.0 | all-reduce | flops 2097152 | bytes 12582912 | tf_op jit(solution)/shard_map/psum | solution.py:26
  482.4 4.4 convert_select_fusion
  486.8 0.0 copy-start.2
  486.8 6.5 copy.13
  493.3 0.0 all-gather.3.cloned.1.call-done
  493.3 0.0 copy-done.2
  493.3 0.0 copy-start.1
  493.3 10.7 %convolution_convert_fusion = bf16[80,2048]{1,0:T(8,128)(2,1)S(1)} fusion(bf16[80,5120]{1,0:T(8,128)(2,1)S(1)} %copy-done.2, bf16[2048,5120]{1,0:T(8,128)(2,1)} %all-gather.3.cloned.1.call-done), kind=kOutput, calls=%fused_computation.1 | convolution fusion | flops 1677885440 | bytes 22118400 | tf_op jit(solution)/shard_map/dot_general | solution.py:12
  504.0 0.0 copy-done.1
  504.0 1.6 convolution_convert_fusion.1
  505.6 0.0 all-gather.5.cloned.1.call-update
  505.6 21.2 %all-gather.5.cloned.1.call-done = bf16[8,80,1024]{2,1,0:T(8,128)(2,1)} async-done(((bf16[2,80,1024]{2,1,0:T(8,128)(2,1)}), bf16[8,80,1024]{2,1,0:T(8,128)(2,1)}) %all-gather.5.cloned.1.call-update) | async-done | bytes 1310736 | tf_op jit(solution)/shard_map/all_gather | solution.py:42
  526.8 0.0 copy-done
  526.8 4.1 fusion.3
  531.0 184.6 %psum.15 = f32[8,8]{1,0:T(8,128)} all-reduce(f32[8,8]{1,0:T(8,128)S(1)} %fusion.3), channel_id=1, replica_groups=mesh['dp'=4,'eig'=64] {'eig'}, use_global_device_ids=true, to_apply=%region_1.2 | all-reduce | flops 64 | bytes 512 | tf_op jit(solution)/shard_map/psum | solution.py:46
  (1 shorter events, 0.0 us)
Async XLA Ops:
  6.5 520.3 %copy-start = (bf16[8,80,1024]{2,1,0:T(8,128)(2,1)S(1)}, bf16[8,80,1024]{2,1,0:T(8,128)(2,1)}, u32[]{:S(2)}) copy-start(bf16[8,80,1024]{2,1,0:T(8,128)(2,1)} %param.13) | copy-start | bytes 3932164
  6.5 486.7 %all-gather.3.cloned.1.call-start = ((), (), s32[]{:S(2)}) async-start(), calls=%async_computation | async-start | bytes 21299200 | tf_op jit(solution)/shard_map/all_gather | solution.py:14
  7.3 519.6 %all-gather.5.cloned.1.call-start = ((), (), s32[]{:S(2)}) async-start(), calls=%async_computation.1 | async-start | bytes 1638400 | tf_op jit(solution)/shard_map/all_gather | solution.py:42
  486.8 6.5 copy-start.2
  493.3 10.7 %copy-start.1 = (bf16[1024,2048]{0,1:T(8,128)(2,1)S(1)}, bf16[1024,2048]{0,1:T(8,128)(2,1)}, u32[]{:S(2)}) copy-start(bf16[1024,2048]{0,1:T(8,128)(2,1)} %copy.13) | copy-start | bytes 12582916
Sparse Core Ops, SparseCore 0:
  11.0 345.3 all-gather.2
  505.7 21.0 all-gather.4
where the time goes:
time: 723 us; the launch traced here: 722 us
  blocking collectives  640 us (89%)
  matrix products  22.2 us (3%)
  waiting for transfers between devices  22 us (3%)
  between operations  18.5 us (3%)
  local copies, waits for them, and re-layouts  14.8 us (2%)
    psum x1, blocking collectives, per_device(): lax.psum(lax.dot_general(chosen_basis, out_grads, (((0,), (0,)), ((), ())...  455 us
    psum x1, blocking collectives, per_device(): return lax.psum(partial_scores, 'eig')  185 us
    all_gather x1, waiting for transfers between devices, per_device(): every_seq = lax.all_gather(seq_grads, 'dp', axis=0, tiled=True)  21.2 us
  transfers between devices with their start and end apart: 2, of which 1 were waited for; matrix products, arithmetic and copies ran while one was open for 4% of the time, Pallas kernels for 0%

commit v1 on v0

--- a/solution.py
+++ b/solution.py
@@ -39,7 +39,9 @@
     seq_grads = jnp.einsum(
         "ksl,isl->sik", grad_blocks, act_blocks, preferred_element_type=jnp.float32
     ).astype(jnp.bfloat16)
-    every_seq = lax.all_gather(seq_grads, "dp", axis=0, tiled=True)
+    every_seq = jnp.concatenate(
+        lax.all_to_all(jnp.stack([seq_grads] * lax.axis_size("dp")), "dp", 0, 0), axis=0
+    )
     partial_scores = jnp.einsum(
         "sik,qik->sq", every_seq, query_grads, preferred_element_type=jnp.float32
     )

time: 723 us -> 712 us (0.985)
  waiting for transfers between devices: 22 us -> 0.71 us
  blocking collectives: 640 us -> 654 us
    all_gather x1 -> x0, waiting for transfers between devices: 21.2 us -> none  [per_device(): every_seq = lax.all_gather(seq_grads, 'dp', axis=0, tiled=True)]
    all_to_all x0 -> x1, blocking collectives: none -> 20.4 us  [per_device(): lax.all_to_all(jnp.stack([seq_grads] * lax.axis_size('dp')), 'dp', 0, 0)]
  transfers between devices with their start and end apart: 2 -> 1, of which waited for: 1 -> 0; matrix products, arithmetic and copies ran while one was open for 4% -> 3% of each run, Pallas kernels for 0% -> 0%
where the time goes in v1:
time: 712 us; the launch traced here: 711 us
  blocking collectives  654 us (92%)
  matrix products  20.3 us (3%)
  between operations  18.5 us (3%)
  local copies, waits for them, and re-layouts  12.2 us (2%)
    psum x1, blocking collectives, per_device(): lax.psum(lax.dot_general(chosen_basis, out_grads, (((0,), (0,)), ((), ())...  454 us
    psum x1, blocking collectives, per_device(): return lax.psum(partial_scores, 'eig')  180 us
    all_to_all x1, blocking collectives, per_device(): lax.all_to_all(jnp.stack([seq_grads] * lax.axis_size('dp')), 'dp', 0, 0)  20.4 us
  transfers between devices with their start and end apart: 1, of which 0 were waited for; matrix products, arithmetic and copies ran while one was open for 3% of the time, Pallas kernels for 0%

profile of v1, /device:TPU:2, one launch (start us, length us, event | category | flops | bytes accessed | tf_op | source)
XLA Modules:
  0.0 711.3 jit_solution(10826067455893197894)
XLA Ops:
  6.5 0.0 copy-start
  6.5 0.0 all-gather.2.cloned.1.call-start
  6.5 0.7 all-gather.2.cloned.1.call-update
  7.3 1.6 fusion.13
  13.9 0.7 iota_compare_fusion
  14.6 0.8 dynamic-slice_dynamic-update-slice_fusion.7
  15.5 0.8 dynamic-slice_dynamic-update-slice_fusion.6
  16.3 0.8 dynamic-slice_dynamic-update-slice_fusion.5
  17.2 0.8 dynamic-slice_dynamic-update-slice_fusion.4
  18.0 0.8 dynamic-slice_dynamic-update-slice_fusion.3
  18.8 0.8 dynamic-slice_dynamic-update-slice_fusion.2
  19.7 0.8 dynamic-slice_dynamic-update-slice_fusion.1
  20.5 0.8 dynamic-slice_dynamic-update-slice_fusion
  21.4 5.8 fusion.14
  27.1 454.2 %all-reduce.1 = bf16[1024,2048]{1,0:T(8,128)(2,1)} all-reduce(f32[1024,2048]{1,0:T(8,128)} %fusion.14), channel_id=1, replica_groups=mesh['dp'=4,'eig'=64] {'eig'}, use_global_device_ids=true, to_apply=%region_0.0 | all-reduce | flops 2097152 | bytes 12582912 | tf_op jit(solution)/shard_map/psum | solution.py:26
  481.3 0.0 copy-start.2
  481.3 4.5 convert_select_fusion
  485.8 0.0 all-gather.2.cloned.1.call-done
  485.8 0.0 copy-done.2
  485.8 0.0 copy-start.1
  485.8 10.7 %convolution_convert_fusion = bf16[80,2048]{1,0:T(8,128)(2,1)S(1)} fusion(bf16[80,5120]{1,0:T(8,128)(2,1)S(1)} %copy-done.2, bf16[2048,5120]{1,0:T(8,128)(2,1)} %all-gather.2.cloned.1.call-done), kind=kOutput, calls=%fused_computation.4 | convolution fusion | flops 1677885440 | bytes 22118400 | tf_op jit(solution)/shard_map/dot_general | solution.py:12
  496.5 0.0 copy-done.1
  496.5 1.4 fusion.5
  497.9 0.3 copy.14
  498.3 0.7 stack.2
  499.0 20.4 %all_to_all.5 = bf16[4,2,80,1024]{3,1,2,0:T(2,128)(2,1)S(1)} all-to-all(bf16[4,2,80,1024]{3,1,2,0:T(2,128)(2,1)S(1)} %stack.2), channel_id=1, replica_groups=mesh['dp'=4,'eig'=64] {'dp'}, dimensions={0} | all-to-all | bytes 2621440 | tf_op jit(solution)/shard_map/all_to_all | solution.py:43
  519.4 1.5 copy.15
  520.9 1.4 reshape.45
  522.3 0.0 copy-done
  522.3 2.4 fusion.8
  524.7 179.8 %psum.15 = f32[8,8]{1,0:T(8,128)} all-reduce(f32[8,8]{1,0:T(8,128)S(1)} %fusion.8), channel_id=1, replica_groups=mesh['dp'=4,'eig'=64] {'eig'}, use_global_device_ids=true, to_apply=%region_1.2 | all-reduce | flops 64 | bytes 512 | tf_op jit(solution)/shard_map/psum | solution.py:48
  (1 shorter events, 0.0 us)
Async XLA Ops:
  6.5 515.7 %copy-start = (bf16[8,80,1024]{2,1,0:T(8,128)(2,1)S(1)}, bf16[8,80,1024]{2,1,0:T(8,128)(2,1)}, u32[]{:S(2)}) copy-start(bf16[8,80,1024]{2,1,0:T(8,128)(2,1)} %param.13) | copy-start | bytes 3932164
  6.5 479.3 %all-gather.2.cloned.1.call-start = ((), (), s32[]{:S(2)}) async-start(), calls=%async_computation.1 | async-start | bytes 21299200 | tf_op jit(solution)/shard_map/all_gather | solution.py:14
  481.3 4.5 copy-start.2
  485.8 10.7 %copy-start.1 = (bf16[1024,2048]{1,0:T(8,128)(2,1)S(1)}, bf16[1024,2048]{1,0:T(8,128)(2,1)}, u32[]{:S(2)}) copy-start(bf16[1024,2048]{1,0:T(8,128)(2,1)} %convert_select_fusion) | copy-start | bytes 12582916
Sparse Core Ops, SparseCore 0:
  11.0 344.7 all-gather.1
